TPU v7x, 256 devices: a whole 4x4x8 slice. The times are simulated.
256 devices in a mesh: ctx: 64 (over y, x, z_hi, core), head: 4 (over z_lo).
Axes of the slice: x: 4, y: 4, z: 8 (z_hi: 2, z_lo: 4; z = z_hi * 4 + z_lo), core: 2. Of those that a mesh axis runs over, the one named last changes fastest.
Arguments:
- streams: bfloat16 [3, 8192, 4096], P(None, 'ctx', 'head'), may hold values from -6 to 6
- short_taps: float32 [3, 7, 4096], P(None, None, 'head'), may hold values from -2 to 2
- long_taps: float32 [256, 128], P('head'), may hold values from -0.5 to 0.5
- skip_gain: float32 [4096], P('head'), may hold values from -4 to 4
- norm_gain: float32 [4096], replicated, may hold values from 0.5 to 8
- w_qkv: bfloat16 [4096, 3, 2048], P('ctx', None, 'head'), may hold values from -0.09375 to 0.09375
Outputs:
- attended: bfloat16 [8192, 2048], P('ctx', 'head')
All inputs are finite; a program needn't handle non-finite values.
Results may differ from a plain program's by a relative error of at most 0.035.
The roundings to bfloat16 on the way count: a program that leaves them out, or rounds other values in their place, can miss the bound.
Values may be sent and summed in bfloat16 or wider, within the bound.
A program may use at most 128 MiB of HBM per device.

v0:
```python
import math

import jax
import jax.numpy as jnp
from jax import lax
from jax.sharding import PartitionSpec as P

HD = 128


def passed_along(x, axis, by):
    size = lax.axis_size(axis)
    pairs = [(i, i + by) for i in range(size) if 0 <= i + by < size]
    return lax.ppermute(x, axis, pairs)


def absorb(state, rows_q, positions, key_heads, value_heads, key_pos, heads):
    running, total, summed = state
    count = rows_q.shape[0]
    query_heads = rows_q.reshape(count, heads, HD)
    scores = jnp.einsum("qhd,khd->hqk", query_heads, key_heads, preferred_element_type=jnp.float32)
    scores = scores * (1.0 / math.sqrt(HD))
    visible = key_pos[None, None, :] <= positions[None, :, None]
    scores = jnp.where(visible, scores, -1e30)
    newest = jnp.maximum(running, jnp.max(scores, axis=-1))
    weights = jnp.where(visible, jnp.exp(scores - newest[:, :, None]), 0.0)
    total = jnp.sum(weights, axis=-1)
    summed = jnp.einsum(
        "hqk,khd->hqd",
        weights.astype(jnp.bfloat16),
        value_heads,
        preferred_element_type=jnp.float32,
    )
    return (newest, total, summed)


def finish(state, heads):
    running, total, summed = state
    count = summed.shape[1]
    result = summed / total[:, :, None]
    return jnp.transpose(result, (1, 0, 2)).reshape(count, heads * HD).astype(jnp.bfloat16)


def per_device(streams, short_taps, long_taps, skip_gain, norm_gain, w_qkv):
    tok_rows = streams.shape[1]
    channels = streams.shape[2]
    short_len = short_taps.shape[1]
    long_len = long_taps.shape[1]
    filters = long_taps.shape[0]
    rim = passed_along(streams[:, tok_rows - (short_len - 1) :], "ctx", 1)
    extended = jnp.concatenate([rim, streams], axis=1).astype(jnp.float32)
    featured = jnp.zeros((3, tok_rows, channels), jnp.float32)
    for offset in range(short_len):
        begin = short_len - 1 - offset
        featured = (
            featured + short_taps[:, offset][:, None, :] * extended[:, begin : begin + tok_rows]
        )
    gated = featured[1] * featured[2]
    gated_rim = passed_along(gated[tok_rows - (long_len - 1) :], "ctx", 1)
    num_blocks = tok_rows // long_len
    gated_ext = jnp.concatenate([gated_rim, gated, jnp.zeros((1, channels), jnp.float32)], axis=0)
    pieces = gated_ext.reshape(num_blocks + 1, long_len, channels)
    windows = jnp.concatenate([pieces[:-1], pieces[1:]], axis=1)
    width = 2 * long_len
    reversed_taps = long_taps[:, ::-1]
    padded_row = jnp.concatenate(
        [reversed_taps, jnp.zeros((filters, width + 1 - long_len), jnp.float32)], axis=1
    )
    toeplitz = jnp.tile(padded_row, (1, long_len))[:, : long_len * width].reshape(
        filters, long_len, width
    )
    grouped = windows.reshape(num_blocks, width, filters, channels // filters)
    conv = jnp.einsum("gts,bsgc->btgc", toeplitz, grouped, precision=lax.Precision.HIGHEST).reshape(
        tok_rows, channels
    )
    mixed = (featured[0] * (conv + skip_gain[None, :] * gated)).astype(jnp.bfloat16)
    whole = lax.all_gather(mixed, "head", axis=1, tiled=True)
    wide = whole.astype(jnp.float32)
    power = jnp.mean(wide * wide, axis=-1, keepdims=True)
    normed = (wide * lax.rsqrt(power + 1e-06) * norm_gain[None, :]).astype(jnp.bfloat16)
    proj = jnp.einsum(
        "td,dkc->tkc",
        normed,
        lax.all_gather(w_qkv, "ctx", axis=0, tiled=True),
        preferred_element_type=jnp.float32,
    )
    proj = proj.astype(jnp.bfloat16)
    query = proj[:, 0]
    keys = proj[:, 1]
    values = proj[:, 2]
    head_cols = query.shape[1]
    heads = head_cols // HD
    device = lax.axis_index("ctx")
    groups = [(query, device * tok_rows + jnp.arange(tok_rows, dtype=jnp.int32))]
    rows_q, positions = groups[0]
    count = rows_q.shape[0]
    starts = [
        (
            jnp.full((heads, count), -1e30, jnp.float32),
            jnp.zeros((heads, count), jnp.float32),
            jnp.zeros((heads, count, HD), jnp.float32),
        )
    ]
    carries = tuple(starts)
    start = jnp.int32(0)
    key_piece = lax.all_gather(keys, "ctx", axis=0, tiled=True)
    value_piece = lax.all_gather(values, "ctx", axis=0, tiled=True)
    rows = key_piece.shape[0]
    key_pos = jnp.arange(rows, dtype=jnp.int32)
    key_heads = key_piece.reshape(rows, heads, HD)
    value_heads = value_piece.reshape(rows, heads, HD)
    updated = []
    for state, group in zip(carries, groups):
        rows_q, positions = group

        def work(current):
            return absorb(current, rows_q, positions, key_heads, value_heads, key_pos, heads)

        def keep(current):
            return current

        updated.append(lax.cond(start <= positions[-1], work, keep, state))
    states = tuple(updated)
    return finish(states[0], heads)


def solution(mesh):
    in_specs = (
        P(None, "ctx", "head"),
        P(None, None, "head"),
        P("head", None),
        P("head"),
        P(),
        P("ctx", None, "head"),
    )
    out_specs = P("ctx", "head")
    return jax.shard_map(
        per_device, mesh=mesh, in_specs=in_specs, out_specs=out_specs, check_vma=False
    )
```

profile of v0, /device:TPU:1, one launch (start us, length us, event | category | flops | bytes accessed | tf_op | source)
XLA Modules:
  0.0 500.6 jit_solution(15351667578578266554)
XLA Ops:
  6.5 0.8 slice.88
  7.4 10.2 %collective-permute-start = (bf16[3,6,1024]{2,1,0:T(8,128)(2,1)S(1)}, bf16[3,6,1024]{2,1,0:T(8,128)(2,1)S(1)}, u32[]{:S(2)}, u32[]{:S(2)}) collective-permute-start(bf16[3,6,1024]{2,1,0:T(8,128)(2,1)S(1)} %slice.88), channel_id=1, source_target_pairs={{0,4},{4,8},{8,12},{12,16},{16,20},{20,24},{24,28},{28,32},{32,36}... | collective-permute-start | bytes 110600 | tf_op jit(solution)/shard_map/ppermute | solution.py:14
  17.6 1.3 fusion.38
  19.1 1.4 maximum_convert_fusion
  20.5 1.3 fusion.20
  21.9 8.3 %collective-permute-start.1 = (f32[127,1024]{1,0:T(8,128)S(1)}, f32[127,1024]{1,0:T(8,128)}, u32[]{:S(2)}, u32[]{:S(2)}) collective-permute-start(f32[127,1024]{1,0:T(8,128)S(1)} %slice_bitcast_fusion), channel_id=1, source_target_pairs={{0,4},{4,8},{8,12},{12,16},{16,20},{20,24},{24,28},{28,32},{32,36}... | collective-permute-start | bytes 1560584 | tf_op jit(solution)/shard_map/ppermute | solution.py:14
  30.3 5.3 %tile.4 = f32[64,128,257]{2,1,0:T(8,128)} broadcast(f32[64,257]{1,0:T(8,128)S(1)} %concatenate.27), dimensions={0,2} | broadcast | bytes 8487168 | tf_op jit(solution)/shard_map/tile | solution.py:69
  35.6 12.2 %tile.10 = f32[64,32896]{1,0:T(8,128)} reshape(f32[64,128,257]{2,1,0:T(8,128)} %tile.4) | data formatting | bytes 16842752 | tf_op jit(solution)/shard_map/tile | solution.py:69
  47.8 3.4 slice-done
  51.2 5.7 %copy.33 = f32[8,8,128,256]{3,2,1,0:T(8,128)} copy(f32[8,8,128,256]{3,1,2,0:T(8,128)S(1)} %bitcast.70) | data formatting | bytes 16777216
  57.0 1.1 pad_maximum_fusion
  58.6 9.3 %fusion.28 = f32[64,16,128]{2,1,0:T(8,128)S(1)} fusion(f32[64,128,256]{2,1,0:T(8,128)} %bitcast.71, f32[1,128,64,16]{1,3,2,0:T(8,128)S(1)} %bitcast.74, f32[1,128,64,16]{1,3,2,0:T(8,128)S(1)} %bitcast.73), kind=kOutput, calls=%fused_computation.41 | convolution fusion | flops 402915328 | bytes 9961472 | tf_op jit(solution)/shard_map/gts,bsgc->btgc/dot_general | solution.py:73
  67.9 0.2 copy.19
  68.1 0.9 fusion.34
  69.0 0.7 all-gather.9.cloned.1.call-update
  69.7 0.2 all-gather.11.cloned.1.call-start
  69.9 30.7 %all-gather.7.cloned.1.call-done = bf16[128,4096]{1,0:T(8,128)(2,1)} async-done(((bf16[128,1024]{1,0:T(8,128)(2,1)}), bf16[128,4096]{1,0:T(8,128)(2,1)}) %all-gather.7.cloned.1.call-update) | async-done | bytes 1048592 | tf_op jit(solution)/shard_map/all_gather | solution.py:77
  100.6 1.5 fusion.17
  102.2 136.0 %all-gather.9.cloned.1.call-done = bf16[4096,3,512]{2,0,1:T(8,128)(2,1)} async-done(((bf16[64,3,512]{2,0,1:T(8,128)(2,1)}), bf16[4096,3,512]{2,0,1:T(8,128)(2,1)}) %all-gather.9.cloned.1.call-update) | async-done | bytes 12582928 | tf_op jit(solution)/shard_map/all_gather | solution.py:84
  238.1 6.8 %convolution_convert_fusion = bf16[128,3,512]{2,0,1:T(8,128)(2,1)S(1)} fusion(bf16[4096,3,512]{2,0,1:T(8,128)(2,1)} %all-gather.9.cloned.1.call-done, bf16[128,4096]{1,0:T(8,128)(2,1)} %all-gather.7.cloned.1.call-done, f32[4096]{0:T(1024)S(1)} %copy-done.1, f32[128]{0:T(128)S(1)} %add_rsqrt_fusion), kind=kOutput, calls=%fused_computation.38 | convolution fusion | flops 1612906496 | bytes 14041600 | tf_op jit(solution)/shard_map/td,dkc->tkc/dot_general | solution.py:81
  244.9 0.7 fusion.37
  245.7 0.5 all-gather.13.cloned.1.call-update
  246.2 0.6 slice.86
  247.6 105.4 %all-gather.11.cloned.1.call-done = bf16[8192,1,512]{2,0,1:T(8,128)(2,1)} async-done(((bf16[128,1,512]{2,0,1:T(8,128)(2,1)}), bf16[8192,1,512]{2,0,1:T(8,128)(2,1)}) %all-gather.11.cloned.1.call-update) | async-done | bytes 8388624 | tf_op jit(solution)/shard_map/all_gather | solution.py:106
  353.0 110.2 %all-gather.13.cloned.1.call-done = bf16[8192,1,512]{2,0,1:T(8,128)(2,1)} async-done(((bf16[128,1,512]{2,0,1:T(8,128)(2,1)}), bf16[8192,1,512]{2,0,1:T(8,128)(2,1)}) %all-gather.13.cloned.1.call-update) | async-done | bytes 8388624 | tf_op jit(solution)/shard_map/all_gather | solution.py:107
  463.2 30.1 %conditional.1 = (f32[4,128]{1,0:T(4,128)S(1)}, f32[4,128,128]{2,1,0:T(8,128)S(1)}) conditional(s32[]{:T(128)} %bitcast.1, () %tuple.13, (s32[8192]{0:T(1024)S(1)}, s32[128]{0:T(128)S(1)}, bf16[128,3,512]{2,0,1:T(8,128)(2,1)S(1)}, bf16[8192,512]{1,0:T(8,128)(2,1)}, bf16[8192,512]{1,0:T(8,128)(2,1)}) %tuple.40), branch_computations={%region_1.0_spmd, %region_2.5_spmd} | conditional | flops 2203057664 | bytes 72790544 | solution.py:122
  463.2 0.6 broadcast_compare_fusion
  463.8 0.2 copy.20
  464.1 9.9 %fusion = (f32[4,128]{1,0:T(4,128)S(1)}, f32[4,128,8192]{2,1,0:T(8,128)}) fusion(pred[128,8192]{1,0:T(8,128)(4,1)S(1)} %broadcast_compare_fusion, bf16[128,4,128]{0,2,1:T(8,128)(2,1)S(1)} %bitcast.76, bf16[8192,512]{1,0:T(8,128)(2,1)} %get-tuple-element.21), kind=kOutput, calls=%fused_computation.2 | convolution fusion | flops 1086324224 | bytes 26347520 | tf_op jit(solution)/shard_map/cond/branch_1_fun/qhd,khd->hqk/dot_general | solution.py:21
  474.0 10.9 %fusion.3 = f32[4,128,128]{2,1,0:T(8,128)S(1)} fusion(f32[4,128,8192]{2,1,0:T(8,128)} %get-tuple-element.38, f32[4,128]{1,0:T(4,128)S(1)} %broadcast_maximum_fusion, pred[128,8192]{1,0:T(8,128)(4,1)S(1)} %broadcast_compare_fusion, bf16[8192,512]{1,0:T(8,128)(2,1)} %get-tuple-element.22), kind=kOutput, calls=%fused_computation.5 | convolution fusion | flops 1094713344 | bytes 26478592 | tf_op jit(solution)/shard_map/cond/branch_1_fun/hqk,khd->hqd/dot_general | solution.py:28
  484.9 8.4 %fusion.2 = f32[4,128]{1,0:T(4,128)S(1)} fusion(f32[4,128,8192]{2,1,0:T(8,128)} %get-tuple-element.38, f32[4,128]{1,0:T(4,128)S(1)} %broadcast_maximum_fusion, pred[128,8192]{1,0:T(8,128)(4,1)S(1)} %broadcast_compare_fusion), kind=kLoop, calls=%fused_computation.4 | loop fusion | flops 20971008 | bytes 17829888 | tf_op jit(solution)/shard_map/cond/branch_1_fun/reduce_sum | solution.py:27
  493.3 0.8 copy_bitcast_fusion
  (30 shorter events, 1.0 us)
Async XLA Ops:
  6.5 94.1 %all-gather.7.cloned.1.call-start = ((), (), s32[]{:S(2)}) async-start(), calls=%async_computation | async-start | bytes 1310720 | tf_op jit(solution)/shard_map/all_gather | solution.py:77
  7.4 11.8 %collective-permute-start = (bf16[3,6,1024]{2,1,0:T(8,128)(2,1)S(1)}, bf16[3,6,1024]{2,1,0:T(8,128)(2,1)S(1)}, u32[]{:S(2)}, u32[]{:S(2)}) collective-permute-start(bf16[3,6,1024]{2,1,0:T(8,128)(2,1)S(1)} %slice.88), channel_id=1, source_target_pairs={{0,4},{4,8},{8,12},{12,16},{16,20},{20,24},{24,28},{28,32},{32,36}... | collective-permute-start | bytes 110600 | tf_op jit(solution)/shard_map/ppermute | solution.py:14
  19.0 11.2 %copy-start = (f32[64,128]{1,0:T(8,128)S(1)}, f32[64,128]{1,0:T(8,128)}, u32[]{:S(2)}) copy-start(f32[64,128]{1,0:T(8,128)} %param.10) | copy-start | bytes 98308
  21.9 35.1 %collective-permute-start.1 = (f32[127,1024]{1,0:T(8,128)S(1)}, f32[127,1024]{1,0:T(8,128)}, u32[]{:S(2)}, u32[]{:S(2)}) collective-permute-start(f32[127,1024]{1,0:T(8,128)S(1)} %slice_bitcast_fusion), channel_id=1, source_target_pairs={{0,4},{4,8},{8,12},{12,16},{16,20},{20,24},{24,28},{28,32},{32,36}... | collective-permute-start | bytes 1560584 | tf_op jit(solution)/shard_map/ppermute | solution.py:14
  47.8 3.4 slice-start
  56.9 11.1 %copy-start.2 = (f32[1024]{0:T(1024)S(1)}, f32[1024]{0:T(1024)}, u32[]{:S(2)}) copy-start(f32[1024]{0:T(1024)} %param.11) | copy-start | bytes 12292
  58.1 180.0 %copy-start.1 = (f32[4096]{0:T(1024)S(1)}, f32[4096]{0:T(1024)}, u32[]{:S(2)}) copy-start(f32[4096]{0:T(1024)} %param.12) | copy-start | bytes 49156
  69.0 169.2 %all-gather.9.cloned.1.call-start = ((), (), s32[]{:S(2)}) async-start(), calls=%async_computation.1 | async-start | bytes 12779520 | tf_op jit(solution)/shard_map/all_gather | solution.py:84
  69.7 283.3 %all-gather.11.cloned.1.call-start = ((), (), s32[]{:S(2)}) async-start(), calls=%async_computation.2 | async-start | bytes 8519680 | tf_op jit(solution)/shard_map/all_gather | solution.py:106
  245.6 217.5 %all-gather.13.cloned.1.call-start = ((), (), s32[]{:S(2)}) async-start(), calls=%async_computation.3 | async-start | bytes 8519680 | tf_op jit(solution)/shard_map/all_gather | solution.py:107
Sparse Core Ops, SparseCore 0:
  69.1 31.5 all-gather.6
  104.2 133.9 all-gather.8
  245.8 107.1 all-gather.10
  356.3 106.7 all-gather.12
where the time goes:
time: 501 us
  waiting for transfers between devices  384 us (77%)
  matrix products  36.9 us (7%)
  local copies, waits for them, and re-layouts  31.1 us (6%)
  starting transfers between devices  18.8 us (4%)
  other arithmetic  16.1 us (3%)
  between operations  14 us (3%)
    all_gather x1, waiting for transfers between devices, per_device(): lax.all_gather(w_qkv, 'ctx', axis=0, tiled=True)  136 us
    all_gather x1, waiting for transfers between devices, per_device(): value_piece = lax.all_gather(values, 'ctx', axis=0, tiled=True)  110 us
    all_gather x1, waiting for transfers between devices, per_device(): key_piece = lax.all_gather(keys, 'ctx', axis=0, tiled=True)  105 us
    all_gather x1, waiting for transfers between devices, per_device(): whole = lax.all_gather(mixed, 'head', axis=1, tiled=True)  30.7 us
    ppermute x2, starting transfers between devices, passed_along(): return lax.ppermute(x, axis, pairs)  18.5 us
    another operation x2, local copies, waits for them, and re-layouts, per_device(): jnp.tile(padded_row, (1, long_len))[:, :long_len * width]  17.5 us
    dot_general x1, matrix products, absorb(): jnp.einsum('hqk,khd->hqd', weights.astype(jnp.bfloat16), value_heads, pre...  10.9 us
  transfers between devices with their start and end apart: 6, of which 5 were waited for; matrix products, arithmetic and copies ran while one was open for 5% of the time, Pallas kernels for 0%

commit v1 on v0

v1 whole, which is shorter than its diff:
```python
import math

import jax
import jax.numpy as jnp
from jax import lax
from jax.experimental import pallas as pl
from jax.experimental.pallas import tpu as pltpu
from jax.sharding import PartitionSpec as P

HD = 128
TOK = 128
HALF = TOK // 2
UNIT = HALF // 2
CH = 1024
SUP = 512
SHORT = 7
GROUP = 16
MESH = pl.DeviceIdType.MESH
BF = jnp.bfloat16
F32 = jnp.float32


def kernel(
    x_ref, st_ref, taps_ref, skip_ref, gain_ref, w_ref, out_ref,
    rim, ext, ghl, gf, x1f, base, thi, tlo, mall, wsrc, wbuf, kv, qt, acc, lsum, mrow, psum, pacc, att, oland,
    s_halo, r_halo, s_w0, r_w0, s_w, r_w, s_kv, r_kv, s_zp, r_zp, s_zm, r_zm, s_oc, r_oc, s_out, r_out,
):
    c = lax.axis_index("ctx")
    zl = lax.axis_index("head")
    s = c // 4
    r = c % 4
    y, x = s // 4, s % 4
    zh, core = r // 2, r % 2
    z = zh * 4 + zl

    def dev(yy, xx, zz, cc):
        return (((yy * 4 + xx) * 2 + zz // 4) * 2 + cc, zz % 4)

    x_next, x_prev = dev(y, (x + 1) % 4, z, core), dev(y, (x + 3) % 4, z, core)
    y_next, y_prev = dev((y + 1) % 4, x, z, core), dev((y + 3) % 4, x, z, core)
    z_next, z_prev = dev(y, x, (z + 1) % 8, core), dev(y, x, (z + 7) % 8, core)
    other = dev(y, x, z, 1 - core)
    x_far, y_far = dev(y, (x + 2) % 4, z, core), dev((y + 2) % 4, x, z, core)
    mate_at = [(zh, 1 - core), (1 - zh, core), (1 - zh, 1 - core)]
    mate_rank = [a * 2 + b for a, b in mate_at]
    mates = [(s * 4 + rank, zl) for rank in mate_rank]
    c_next, c_prev = ((c + 1) % 64, zl), ((c + 63) % 64, zl)

    pending = []

    def send(src, dst, s_sem, r_sem, to):
        copy = pltpu.make_async_remote_copy(
            src_ref=src, dst_ref=dst, send_sem=s_sem, recv_sem=r_sem, device_id=to, device_id_type=MESH
        )
        copy.start()
        pending.append(copy)

    def recv(dst, s_sem, r_sem, frm):
        pltpu.make_async_remote_copy(
            src_ref=dst, dst_ref=dst, send_sem=s_sem, recv_sem=r_sem, device_id=frm, device_id_type=MESH
        ).wait_recv()

    barrier = pltpu.get_barrier_semaphore()
    partners = [x_next, x_prev, y_next, y_prev, z_next, z_prev, c_next, c_prev, x_far, y_far] + mates
    for p in partners:
        pl.semaphore_signal(barrier, inc=1, device_id=p, device_id_type=MESH)

    for rr in range(4):
        for k in range(3):
            wsrc[rr, :, k * HD : (k + 1) * HD] = w_ref[k, :, rr * HD : (rr + 1) * HD]

    def own_slot(h):
        return (1 - h) * (y * 4 + x) + h * (x * 4 + y)

    pl.semaphore_wait(barrier, len(partners))
    send(x_ref.at[:, pl.ds(TOK - 16, 16), :], rim, s_halo.at[3], r_halo.at[3], c_next)
    mine = wbuf.at[zh, core, own_slot(core)]
    for k in range(3):
        send(wsrc.at[mate_rank[k]], mine, s_w0.at[k], r_w0.at[k], mates[k])
    wbuf[zh, core, own_slot(core)] = wsrc[r]

    def weights_from(k):
        zz, cc = mate_at[k]
        recv(wbuf.at[zz, cc, own_slot(cc)], s_w0.at[k], r_w0.at[k], mates[k])

    def fill(stream, _):
        ext[stream, 16:, :] = x_ref[stream].astype(F32)
        return 0

    lax.fori_loop(0, 3, fill, 0)

    def featured(stream, lo, hi, lanes):
        total = None
        for j in range(SHORT):
            term = st_ref[stream, pl.ds(j, 1), lanes] * ext[stream, pl.ds(16 + lo - j, hi - lo), lanes]
            total = term if total is None else total + term
        return total

    def gate_rows(lo, hi):
        def slab(i, _):
            lanes = pl.ds(pl.multiple_of(i * 128, 128), 128)
            gated = featured(1, lo, hi, lanes) * featured(2, lo, hi, lanes)
            gf[lo:hi, lanes] = gated
            high = gated.astype(BF)
            ghl[i, TOK + lo : TOK + hi, :128] = high
            ghl[i, TOK + lo : TOK + hi, 128:] = (gated - high.astype(F32)).astype(BF)
            return 0
        lax.fori_loop(0, CH // 128, slab, 0)

    def x1_rows(lo, hi):
        def slab(i, _):
            lanes = pl.ds(pl.multiple_of(i * 128, 128), 128)
            x1f[lo:hi, lanes] = featured(0, lo, hi, lanes)
            return 0
        lax.fori_loop(0, CH // 128, slab, 0)

    def gated_rows(lo, count, block):
        return ghl.at[:, pl.ds(TOK * block + lo, count), pl.ds(0, 128)]

    halo = ((HALF, HALF), (16, HALF - 16), (0, 16))

    def halo_send(k):
        send(gated_rows(*halo[k], 1), gated_rows(*halo[k], 0), s_halo.at[k], r_halo.at[k], c_next)

    def halo_recv(k):
        recv(gated_rows(*halo[k], 0), s_halo.at[k], r_halo.at[k], c_prev)

    gate_rows(HALF, TOK)
    halo_send(0)

    def gather_steps(buf, s_sem, r_sem):
        mid = buf.shape[2] // 2

        def parts(h):
            if h == 0:
                return x, y, x_next, x_prev, y_next, y_prev, x_far
            return y, x, y_next, y_prev, x_next, x_prev, y_far

        def slot(a, b):
            return (b % 4) * 4 + a % 4

        def whole(h, a, b):
            return buf.at[h, slot(a, b)]

        def piece(h, a, b, p):
            return buf.at[h, slot(a, b), pl.ds(p * mid, mid), :]

        def go(h, ref, idx, to):
            send(ref, ref, s_sem.at[h, idx], r_sem.at[h, idx], to)

        def come(h, ref, idx, frm):
            recv(ref, s_sem.at[h, idx], r_sem.at[h, idx], frm)

        off = (0, -1, 1, 2)

        def spread(h, i):
            a, b, fn, fp, gn, gp, ff = parts(h)
            ref = whole(h, a + off[i] + 4, b)
            go(h, ref, 4 + i, gn)
            go(h, ref, 8 + i, gp)

        def start():
            for h in (0, 1):
                a, b, fn, fp, gn, gp, ff = parts(h)
                go(h, whole(h, a, b), 0, fn)
                go(h, whole(h, a, b), 1, fp)
                go(h, whole(h, a, b), 2, ff)
            for h in (0, 1):
                spread(h, 0)

        def near():
            for h in (0, 1):
                a, b, fn, fp, gn, gp, ff = parts(h)
                come(h, whole(h, a + 3, b), 0, fp)
                come(h, whole(h, a + 1, b), 1, fn)
            for h in (0, 1):
                spread(h, 1)
                spread(h, 2)

        def far():
            for h in (0, 1):
                a, b, fn, fp, gn, gp, ff = parts(h)
                come(h, whole(h, a + 2, b), 2, ff)
                spread(h, 3)

        def across(i):
            for h in (0, 1):
                a, b, fn, fp, gn, gp, ff = parts(h)
                aa = a + off[i] + 4
                come(h, whole(h, aa, b + 3), 4 + i, gp)
                go(h, piece(h, aa, b + 3, 0), 12 + i, gn)
                come(h, whole(h, aa, b + 1), 8 + i, gn)
                go(h, piece(h, aa, b + 1, 1), 16 + i, gp)

        def last(i):
            for h in (0, 1):
                a, b, fn, fp, gn, gp, ff = parts(h)
                aa = a + off[i] + 4
                come(h, piece(h, aa, b + 2, 0), 12 + i, gp)
                come(h, piece(h, aa, b + 2, 1), 16 + i, gn)

        return start, near, far, across, last

    a_start, a_near, a_far, a_across, a_last = gather_steps(wbuf.at[zh], s_w.at[0], r_w.at[0])
    b_start, b_near, b_far, b_across, b_last = gather_steps(wbuf.at[1 - zh], s_w.at[1], r_w.at[1])

    weights_from(0)
    a_start()
    gate_rows(16, HALF)
    halo_send(1)
    x1_rows(16, TOK)

    def clear(i, _):
        ghl[i, :TOK, 128:] = jnp.zeros((TOK, 128), BF)
        ghl[i, 2 * TOK :, :] = jnp.zeros((HALF, 256), BF)
        return 0

    lax.fori_loop(0, CH // 128, clear, 0)

    turn = lax.broadcasted_iota(jnp.int32, (128, 256), 0) + lax.broadcasted_iota(jnp.int32, (128, 256), 1)
    turn = jnp.where(turn == 128, 1.0, 0.0).astype(BF)
    taps = taps_ref[...]
    taps_high = taps.astype(BF)
    taps_low = (taps - taps_high.astype(F32)).astype(BF)
    base[...] = jnp.dot(taps_high, turn, preferred_element_type=F32) + jnp.dot(
        taps_low, turn, preferred_element_type=F32
    )

    def build(g, _):
        row = jnp.broadcast_to(base[pl.ds(g, 1), :], (HALF, 256))
        rows = pl.ds(pl.multiple_of(g * HALF, HALF), HALF)
        rolled = pltpu.roll(row, 0, 1, stride=1, stride_axis=0)
        high = rolled.astype(BF)
        thi[rows, :] = high
        tlo[rows, :] = (rolled - high.astype(F32)).astype(BF)
        return 0

    lax.fori_loop(0, CH // GROUP, build, 0)

    lane_group = lax.broadcasted_iota(jnp.int32, (HALF, 128), 1) // GROUP
    per = 128 // GROUP

    def convolve(half):
        for k in (0,) if half == 0 else (1, 2):
            halo_recv(k)
        lo = HALF * (1 - half)

        @pl.when(first)
        def _():
            ghl[:, lo : lo + HALF, :128] = jnp.zeros((CH // 128, HALF, 128), BF)

        window = slice(lo, lo + 256)

        def slab(i, _):
            rows = pl.ds(pl.multiple_of(i * per * HALF, per * HALF), per * HALF)
            both = jnp.dot(thi[rows, :], ghl[i, window, :], preferred_element_type=F32)
            rest = jnp.dot(tlo[rows, :], ghl[i, window, :128], preferred_element_type=F32)
            both = both[:, :128] + both[:, 128:] + rest
            conv = both[:HALF]
            for g in range(1, per):
                conv = jnp.where(lane_group == g, both[g * HALF : (g + 1) * HALF], conv)
            lanes = pl.ds(pl.multiple_of(i * 128, 128), 128)
            mixed = x1f[lo : lo + HALF, lanes] * (conv + skip_ref[:, lanes] * gf[lo : lo + HALF, lanes])
            mall[half, zl, pl.ds(pl.multiple_of(r * HALF, HALF), HALF), lanes] = mixed.astype(BF)
            return 0

        lax.fori_loop(0, CH // 128, slab, 0)

    def origin(half, zz, cc, u):
        zz = zz % 8
        return mall.at[half, zz % 4, pl.ds(((zz // 4) * 2 + cc) * HALF + u * UNIT, UNIT), :]

    def square(half, zz, cc, u):
        zz = zz % 8
        at = pl.ds(pl.multiple_of(((zz // 4) * 2 + cc) * HALF + u * UNIT, UNIT), UNIT)
        m = mall[half, zz % 4, at, :].astype(F32)
        m = m * m
        total = m[:, :128]
        for i in range(1, CH // 128):
            total = total + m[:, i * 128 : (i + 1) * 128]
        psum[at, :] += total

    def ring_own(half):
        for u in (0, 1):
            own = origin(half, z, core, u)
            send(own, own, s_zp.at[half, 0, u], r_zp.at[half, 0, u], z_next)
            send(own, own, s_zm.at[half, 0, u], r_zm.at[half, 0, u], z_prev)
        for u in (0, 1):
            own = origin(half, z, core, u)
            send(own, own, s_oc.at[half, 0, u], r_oc.at[half, 0, u], other)

    def ring_step(half, k):
        for u in (0, 1):
            if k < 3 or u == 0:
                ref = origin(half, z + 7 - k, core, u)
                recv(ref, s_zp.at[half, k, u], r_zp.at[half, k, u], z_prev)
                if k + 1 < 3 or (k + 1 == 3 and u == 0):
                    send(ref, ref, s_zp.at[half, k + 1, u], r_zp.at[half, k + 1, u], z_next)
                send(ref, ref, s_oc.at[half, 1 + k, u], r_oc.at[half, 1 + k, u], other)
            if k < 3 or u == 1:
                ref = origin(half, z + 1 + k, core, u)
                recv(ref, s_zm.at[half, k, u], r_zm.at[half, k, u], z_next)
                if k + 1 < 3 or (k + 1 == 3 and u == 1):
                    send(ref, ref, s_zm.at[half, k + 1, u], r_zm.at[half, k + 1, u], z_prev)
                idx = 5 + k if k < 3 else 4
                send(ref, ref, s_oc.at[half, idx, u], r_oc.at[half, idx, u], other)
        if half == 1 and k < 2:
            return
        for u in (0, 1):
            if k < 3 or u == 0:
                square(half, z + 7 - k, core, u)
            if k < 3 or u == 1:
                square(half, z + 1 + k, core, u)

    def from_other(half, idx, step):
        for u in (0, 1):
            recv(origin(half, z + step, 1 - core, u), s_oc.at[half, idx, u], r_oc.at[half, idx, u], other)
            square(half, z + step, 1 - core, u)

    def project(half, zs):
        inv = lax.rsqrt(jnp.sum(psum[...], axis=-1, keepdims=True) * (1.0 / (4 * CH)) + 1e-06)
        for zz in zs:
            normed = (mall[half, zz].astype(F32) * inv * gain_ref[:, zz * CH : (zz + 1) * CH]).astype(BF)
            pieces = []
            for i in range(4):
                for zhi in (0, 1):
                    pieces += [wbuf[zhi, 0, zz * 4 + i], wbuf[zhi, 1, i * 4 + zz]]
            part = jnp.dot(normed, jnp.concatenate(pieces, axis=0), preferred_element_type=F32)
            if zz == 0:
                pacc[...] = part
            else:
                pacc[...] += part

    def place(half):
        proj = pacc[...].astype(BF).astype(F32)
        qt[:, half * 256 : (half + 1) * 256] = jnp.transpose(proj[:, :HD]).astype(BF)
        values = jnp.transpose(proj[:, 2 * HD :]).astype(BF)
        for h in (0, 1):
            kv[half, h, own_slot(h), :128, :] = proj[h * 128 : (h + 1) * 128, HD : 2 * HD].astype(BF)
            kv[half, h, own_slot(h), 128:, :] = values[:, h * 128 : (h + 1) * 128]

    scale = math.log2(math.e) / math.sqrt(HD)

    def position(index):
        half = lax.shift_right_logical(index, 8)
        return (lax.shift_right_logical(index, 6) & 3) * TOK + (1 - half) * HALF + (index & (HALF - 1))

    def scores_of(half, h, index):
        keys = kv[half, h, index, :128, :]
        return jnp.dot(keys, qt[...], preferred_element_type=F32) * scale

    def weigh(units, probs):
        values = jnp.concatenate([kv[half, h, index, 128:, :] for half, h, index in units], axis=1)
        probs = jnp.concatenate([p.astype(BF) for p in probs], axis=0)
        return jnp.dot(values, probs, preferred_element_type=F32)

    def total_of(probs):
        total = probs[0]
        for p in probs[1:]:
            total = total + p
        return jnp.sum(total, axis=0, keepdims=True)

    def absorb_own():
        units = [(half, h, own_slot(h)) for half in (0, 1) for h in (0, 1)]
        q_pos = position(lax.broadcasted_iota(jnp.int32, (128, SUP), 1))
        scores = []
        for half, h, index in units:
            k_pos = position(lax.broadcasted_iota(jnp.int32, (128, SUP), 0) + (half * 256 + h * 128))
            scores.append(jnp.where(k_pos <= q_pos, scores_of(half, h, index), -1e30))
        top = scores[0]
        for t in scores[1:]:
            top = jnp.maximum(top, t)
        top = jnp.max(top, axis=0, keepdims=True)
        probs = [jnp.exp2(t - top) for t in scores]
        mrow[...] = top
        lsum[...] = total_of(probs)
        acc[...] = weigh(units, probs)

    def absorb(units):
        biases = [jnp.where(block < s, 0.0, -1e30) for _, _, _, block in units]
        units = [unit[:3] for unit in units]
        scores = [scores_of(*unit) for unit in units]
        old = mrow[...]
        top = old
        for t, bias in zip(scores, biases):
            top = jnp.maximum(top, jnp.max(t, axis=0, keepdims=True) + bias)
        probs = [jnp.exp2(t - (top - bias)) for t, bias in zip(scores, biases)]
        alpha = jnp.exp2(old - top)
        mrow[...] = top
        lsum[...] = lsum[...] * alpha + total_of(probs)
        acc[...] = acc[...] * alpha + weigh(units, probs)

    def stored(lo, hi):
        def some(j, _):
            h, jj = j // 4, j % 4
            units = []
            for t in range(4):
                units.append((0, h, jj * 4 + t, (1 - h) * (jj * 4 + t) + h * (t * 4 + jj)))
            lowest = (1 - h) * jj * 4 + h * jj

            @pl.when(lowest < s)
            def _():
                absorb(units)
            return 0
        lax.fori_loop(lo, hi, some, 0)

    def arrived(places):
        units = []
        for h, da, db in places:
            a, b = (x, y) if h == 0 else (y, x)
            aa, bb = (a + da + 4) % 4, (b + db + 4) % 4
            units.append((1, h, bb * 4 + aa, bb * 4 + aa if h == 0 else aa * 4 + bb))
        seen = units[0][3] < s
        for unit in units[1:]:
            seen = seen | (unit[3] < s)

        @pl.when(seen)
        def _():
            absorb(units)

    first = c == 0
    recv(rim, s_halo.at[3], r_halo.at[3], c_prev)
    ext[:, :16, :] = jnp.where(first, 0.0, rim[...].astype(F32))
    gate_rows(0, 16)
    halo_send(2)
    x1_rows(0, 16)
    a_near()
    weights_from(1)
    weights_from(2)
    b_start()
    convolve(0)
    ring_own(0)
    psum[...] = jnp.zeros_like(psum)
    a_far()
    a_across(0)
    square(0, z, core, 0)
    square(0, z, core, 1)
    a_across(1)
    a_across(2)
    ring_step(0, 0)
    b_near()
    b_far()
    b_across(0)
    convolve(1)
    ring_own(1)
    a_across(3)
    ring_step(0, 1)
    from_other(0, 0, 0)
    b_across(1)
    b_across(2)
    ring_step(1, 0)
    ring_step(0, 2)
    from_other(0, 1, 7)
    from_other(0, 5, 1)
    b_across(3)
    ring_step(1, 1)
    from_other(0, 2, 6)
    from_other(0, 6, 2)
    ring_step(0, 3)
    from_other(0, 3, 5)
    from_other(0, 7, 3)
    from_other(0, 4, 4)
    for i in range(4):
        a_last(i)
    for i in range(4):
        b_last(i)
    project(0, (0, 1, 2, 3))
    place(0)
    k0_start, k0_near, k0_far, k0_across, k0_last = gather_steps(kv.at[0], s_kv.at[0], r_kv.at[0])
    k0_start()

    psum[...] = jnp.zeros_like(psum)
    ring_step(1, 2)
    square(1, z, core, 0)
    square(1, z, core, 1)
    for k in (0, 1):
        for u in (0, 1):
            square(1, z + 7 - k, core, u)
            square(1, z + 1 + k, core, u)
    from_other(1, 0, 0)
    from_other(1, 1, 7)
    from_other(1, 5, 1)
    k0_near()
    k0_far()
    k0_across(0)
    from_other(1, 2, 6)
    from_other(1, 6, 2)
    ring_step(1, 3)
    k0_across(1)
    k0_across(2)
    from_other(1, 3, 5)
    from_other(1, 7, 3)
    from_other(1, 4, 4)
    k0_across(3)
    project(1, (0, 1, 2, 3))
    place(1)
    k1_start, k1_near, k1_far, k1_across, k1_last = gather_steps(kv.at[1], s_kv.at[1], r_kv.at[1])
    k1_start()
    absorb_own()
    for i in range(4):
        k0_last(i)
    stored(0, 2)
    k1_near()
    k1_across(0)
    stored(2, 4)
    k1_far()
    stored(4, 6)
    k1_across(1)
    k1_across(2)
    stored(6, 8)
    arrived([(0, -1, 0), (0, 1, 0), (1, -1, 0), (1, 1, 0)])
    k1_across(3)
    arrived([(0, 2, 0), (1, 2, 0)])
    off = (0, -1, 1, 2)
    for i in range(4):
        arrived([(0, off[i], -1), (0, off[i], 1), (1, off[i], -1), (1, off[i], 1)])
    for i in (0, 2):
        k1_last(i)
        k1_last(i + 1)
        arrived([(0, off[i], 2), (0, off[i + 1], 2), (1, off[i], 2), (1, off[i + 1], 2)])

    result = jnp.transpose(acc[...] / lsum[...]).astype(BF)
    for half in (0, 1):
        for rr in range(4):
            lo = half * 256 + rr * HALF
            att[rr, HALF * (1 - half) : HALF * (2 - half), :] = result[lo : lo + HALF]
    for k in range(3):
        send(att.at[mate_rank[k]], oland.at[r], s_out.at[k], r_out.at[k], mates[k])
    oland[r] = att[r]
    for k in range(3):
        recv(oland.at[mate_rank[k]], s_out.at[k], r_out.at[k], mates[k])
    for rr in range(4):
        out_ref[:, rr * HD : (rr + 1) * HD] = oland[rr]
    for copy in pending:
        copy.wait_send()


def per_device(streams, short_taps, long_taps, skip_gain, norm_gain, w_qkv):
    vmem = pl.BlockSpec(memory_space=pltpu.VMEM)
    dma = pltpu.SemaphoreType.DMA
    return pl.pallas_call(
        kernel,
        out_shape=jax.ShapeDtypeStruct((TOK, 4 * HD), BF),
        in_specs=[vmem] * 6,
        out_specs=vmem,
        scratch_shapes=[
            pltpu.VMEM((3, 16, CH), BF),
            pltpu.VMEM((3, 16 + TOK, CH), F32),
            pltpu.VMEM((CH // 128, 2 * TOK + HALF, 256), BF),
            pltpu.VMEM((TOK, CH), F32),
            pltpu.VMEM((TOK, CH), F32),
            pltpu.VMEM((64, 256), F32),
            pltpu.VMEM((CH // GROUP * HALF, 256), BF),
            pltpu.VMEM((CH // GROUP * HALF, 256), BF),
            pltpu.VMEM((2, 4, 256, CH), BF),
            pltpu.VMEM((4, 64, 3 * HD), BF),
            pltpu.VMEM((2, 2, 16, 64, 3 * HD), BF),
            pltpu.VMEM((2, 2, 16, 256, HD), BF),
            pltpu.VMEM((HD, SUP), BF),
            pltpu.VMEM((HD, SUP), F32),
            pltpu.VMEM((1, SUP), F32),
            pltpu.VMEM((1, SUP), F32),
            pltpu.VMEM((256, 128), F32),
            pltpu.VMEM((256, 3 * HD), F32),
            pltpu.VMEM((4, TOK, HD), BF),
            pltpu.VMEM((4, TOK, HD), BF),
            dma((4,)), dma((4,)),
            dma((3,)), dma((3,)),
            dma((2, 2, 20)), dma((2, 2, 20)),
            dma((2, 2, 20)), dma((2, 2, 20)),
            dma((2, 4, 2)), dma((2, 4, 2)),
            dma((2, 4, 2)), dma((2, 4, 2)),
            dma((2, 8, 2)), dma((2, 8, 2)),
            dma((3,)), dma((3,)),
        ],
        compiler_params=pltpu.CompilerParams(
            collective_id=0, has_side_effects=True, vmem_limit_bytes=56 * 1024 * 1024
        ),
    )(
        streams,
        short_taps,
        long_taps,
        skip_gain.reshape(1, CH),
        norm_gain.reshape(1, 4 * CH),
        jnp.transpose(w_qkv, (1, 0, 2)),
    )


def solution(mesh):
    in_specs = (
        P(None, "ctx", "head"),
        P(None, None, "head"),
        P("head", None),
        P("head"),
        P(),
        P("ctx", None, "head"),
    )
    return jax.shard_map(
        per_device, mesh=mesh, in_specs=in_specs, out_specs=P("ctx", "head"), check_vma=False
    )
```

time: 501 us -> 93.4 us (0.19)
  waiting for transfers between devices: 384 us -> 0 us
  Pallas kernels: 0 us -> 91.7 us
  matrix products: 36.9 us -> 0 us
  local copies, waits for them, and re-layouts: 31.1 us -> 1.57 us
  starting transfers between devices: 18.8 us -> 0 us
  other arithmetic: 16.1 us -> 0 us
  between operations: 14 us -> 0.01 us
    all_gather x4 -> x0, waiting for transfers between devices: 382 us -> none  [the longest x1 136 us: per_device(): lax.all_gather(w_qkv, 'ctx', axis=0, tiled=True)]
    pallas_call x0 -> x1, Pallas kernels: none -> 91.7 us  [per_device(): pl.pallas_call(kernel, out_shape=jax.ShapeDtypeStruct((TOK, 4 * HD), BF),...]
    dot_general x4 -> x0, matrix products: 36.9 us -> none  [the longest x1 10.9 us: absorb(): jnp.einsum('hqk,khd->hqd', weights.astype(jnp.bfloat16), value_heads, pre...]
    ppermute x2 -> x0, starting transfers between devices: 18.5 us -> none  [passed_along(): return lax.ppermute(x, axis, pairs)]
    another operation x3 -> x0, local copies, waits for them, and re-layouts: 17.7 us -> none  [the longest x2 17.5 us: per_device(): jnp.tile(padded_row, (1, long_len))[:, :long_len * width]]
    reduce_sum x2 -> x0, other arithmetic: 9.89 us -> none  [the longest x1 8.37 us: absorb(): total = jnp.sum(weights, axis=-1)]
    slice x10 -> x0, local copies, waits for them, and re-layouts: 7.32 us -> none  [the longest x2 3.38 us: per_device(): jnp.tile(padded_row, (1, long_len))[:, :long_len * width]]
  transfers between devices with their start and end apart: 6 -> 0, of which waited for: 5 -> 0; matrix products, arithmetic and copies ran while one was open for 5% -> 0% of each run, Pallas kernels for 0% -> 0%
where the time goes in v1:
time: 93.4 us; the launch traced here: 93.3 us
  Pallas kernels  91.7 us (98%)
  local copies, waits for them, and re-layouts  1.57 us (2%)
    pallas_call x1, Pallas kernels, per_device(): pl.pallas_call(kernel, out_shape=jax.ShapeDtypeStruct((TOK, 4 * HD), BF),...  91.7 us

profile of v1, /device:TPU:1, one launch (start us, length us, event | category | flops | bytes accessed | tf_op | source)
XLA Modules:
  0.0 93.3 jit_solution(4139413359906643839)
XLA Ops:
  0.0 91.7 %shard_map.64 = bf16[128,512]{1,0:T(8,128)(2,1)} custom-call(bf16[3,128,1024]{2,1,0:T(8,128)(2,1)} %x_ref.1, f32[3,7,1024]{2,1,0:T(8,128)} %st_ref.1, f32[64,128]{1,0:T(8,128)} %taps_ref.1, f32[1,1024]{1,0:T(1,128)} %bitcast.5, f32[1,4096]{1,0:T(1,128)} %bitcast.4, bf16[3,64,512]{2,1,0:T(8,128)(2,1)} %bitcast.3), custom_call_target="tpu_custom_call" | custom-call | tf_op jit(solution)/shard_map/pallas_call | solution.py:541
  91.7 1.6 %copy.8 = bf16[128,512]{1,0:T(8,128)(2,1)} copy(bf16[128,512]{1,0:T(8,128)(2,1)} %shard_map.64) | data formatting | bytes 262144

commit v2 on v1

v2 whole, which is shorter than its diff:
```python
import math

import jax
import jax.numpy as jnp
from jax import lax
from jax.experimental import pallas as pl
from jax.experimental.pallas import tpu as pltpu
from jax.sharding import PartitionSpec as P

HD = 128
TOK = 128
HALF = TOK // 2
UNIT = HALF // 2
CH = 1024
SUP = 512
SHORT = 7
GROUP = 16
MESH = pl.DeviceIdType.MESH
BF = jnp.bfloat16
F32 = jnp.float32


def kernel(
    x_hbm, st_ref, taps_ref, skip_ref, gain_ref, w_hbm, out_ref,
    x_ref, w_ref, rim_src, rim, ext, ghl, gf, x1f, base, thi, tlo, mall, wsrc, wbuf, normed, kv, qt, acc, lsum, mrow, psum, att, oland,
    l_in, s_halo, r_halo, s_w0, r_w0, s_w, r_w, s_kv, r_kv, s_zp, r_zp, s_zm, r_zm, s_oc, r_oc, s_out, r_out,
):
    c = lax.axis_index("ctx")
    zl = lax.axis_index("head")
    s = c // 4
    r = c % 4
    y, x = s // 4, s % 4
    zh, core = r // 2, r % 2
    z = zh * 4 + zl

    def dev(yy, xx, zz, cc):
        return (((yy * 4 + xx) * 2 + zz // 4) * 2 + cc, zz % 4)

    x_next, x_prev = dev(y, (x + 1) % 4, z, core), dev(y, (x + 3) % 4, z, core)
    y_next, y_prev = dev((y + 1) % 4, x, z, core), dev((y + 3) % 4, x, z, core)
    z_next, z_prev = dev(y, x, (z + 1) % 8, core), dev(y, x, (z + 7) % 8, core)
    other = dev(y, x, z, 1 - core)
    x_far, y_far = dev(y, (x + 2) % 4, z, core), dev((y + 2) % 4, x, z, core)
    mate_at = [(zh, 1 - core), (1 - zh, core), (1 - zh, 1 - core)]
    mate_rank = [a * 2 + b for a, b in mate_at]
    mates = [(s * 4 + rank, zl) for rank in mate_rank]
    c_next, c_prev = ((c + 1) % 64, zl), ((c + 63) % 64, zl)

    pending = []

    def send(src, dst, s_sem, r_sem, to):
        copy = pltpu.make_async_remote_copy(
            src_ref=src, dst_ref=dst, send_sem=s_sem, recv_sem=r_sem, device_id=to, device_id_type=MESH
        )
        copy.start()
        pending.append(copy)
        return copy

    def recv(dst, s_sem, r_sem, frm):
        pltpu.make_async_remote_copy(
            src_ref=dst, dst_ref=dst, send_sem=s_sem, recv_sem=r_sem, device_id=frm, device_id_type=MESH
        ).wait_recv()

    x_in = pltpu.make_async_copy(x_hbm, x_ref, l_in.at[0])
    x_in.start()
    w_in = pltpu.make_async_copy(w_hbm, w_ref, l_in.at[1])
    w_in.start()

    barrier = pltpu.get_barrier_semaphore()
    partners = [c_next, c_prev] + mates + [x_far, y_far, x_next, x_prev, y_next, y_prev, z_next, z_prev]
    for p in partners:
        pl.semaphore_signal(barrier, inc=1, device_id=p, device_id_type=MESH)

    def own_slot(h):
        return (1 - h) * (y * 4 + x) + h * (x * 4 + y)

    def fill(stream, _):
        ext[stream, 16:, :] = x_ref[stream].astype(F32)
        return 0

    x_in.wait()
    lax.fori_loop(0, 3, fill, 0)

    def featured(stream, lo, hi, lanes):
        total = None
        for j in range(SHORT):
            term = st_ref[stream, pl.ds(j, 1), lanes] * ext[stream, pl.ds(16 + lo - j, hi - lo), lanes]
            total = term if total is None else total + term
        return total

    def gate_rows(lo, hi):
        def slab(i, _):
            lanes = pl.ds(pl.multiple_of(i * 128, 128), 128)
            gated = featured(1, lo, hi, lanes) * featured(2, lo, hi, lanes)
            gf[lo:hi, lanes] = gated
            high = gated.astype(BF)
            ghl[i, TOK + lo : TOK + hi, :128] = high
            ghl[i, TOK + lo : TOK + hi, 128:] = (gated - high.astype(F32)).astype(BF)
            return 0
        lax.fori_loop(0, CH // 128, slab, 0)

    def x1_rows(lo, hi):
        def slab(i, _):
            lanes = pl.ds(pl.multiple_of(i * 128, 128), 128)
            x1f[lo:hi, lanes] = featured(0, lo, hi, lanes)
            return 0
        lax.fori_loop(0, CH // 128, slab, 0)

    def gated_rows(lo, count, block):
        return ghl.at[:, pl.ds(TOK * block + lo, count), pl.ds(0, 128)]

    halo = ((HALF, HALF), (16, HALF - 16), (0, 16))

    def halo_send(k):
        send(gated_rows(*halo[k], 1), gated_rows(*halo[k], 0), s_halo.at[k], r_halo.at[k], c_next)

    def halo_recv(k):
        recv(gated_rows(*halo[k], 0), s_halo.at[k], r_halo.at[k], c_prev)

    gate_rows(HALF, TOK)
    gate_rows(16, HALF)
    x1_rows(16, TOK)

    rows = jnp.concatenate([ext[i, 16 + TOK - 6 :, :] for i in range(3)], axis=0)
    rim_src[:, :CH] = rows[:16].astype(BF)
    rest = jnp.concatenate([rows[16:, i * 128 : (i + 1) * 128] for i in range(8)], axis=0)
    rim_src[:, CH:] = rest.astype(BF)

    w_in.wait()
    for rr in range(4):
        for k in range(3):
            wsrc[rr, :, k * HD : (k + 1) * HD] = w_ref[k, :, rr * HD : (rr + 1) * HD]
    wbuf[zh, core, own_slot(core)] = wsrc[r]

    pl.semaphore_wait(barrier, len(partners))
    send(rim_src, rim, s_halo.at[3], r_halo.at[3], c_next)
    halo_send(0)
    mine = wbuf.at[zh, core, own_slot(core)]

    def weights_to(k):
        send(wsrc.at[mate_rank[k]], mine, s_w0.at[k], r_w0.at[k], mates[k])

    def weights_from(k):
        zz, cc = mate_at[k]
        recv(wbuf.at[zz, cc, own_slot(cc)], s_w0.at[k], r_w0.at[k], mates[k])

    weights_to(0)
    weights_to(1)
    weights_to(2)

    def clear(i, _):
        ghl[i, :TOK, 128:] = jnp.zeros((TOK, 128), BF)
        ghl[i, 2 * TOK :, :] = jnp.zeros((96, 256), BF)
        return 0

    lax.fori_loop(0, CH // 128, clear, 0)
    halo_send(1)

    def gather_steps(buf, s_sem, r_sem):
        mid = buf.shape[2] // 2

        def parts(h):
            first = (x, y, x_next, x_prev, y_next, y_prev, x_far)
            second = (y, x, y_next, y_prev, x_next, x_prev, y_far)
            if isinstance(h, int):
                return second if h else first
            mixed = []
            for p, q in zip(first, second):
                if isinstance(p, tuple):
                    mixed.append(tuple(i * (1 - h) + j * h for i, j in zip(p, q)))
                else:
                    mixed.append(p * (1 - h) + q * h)
            return mixed

        def slot(a, b):
            return (b % 4) * 4 + a % 4

        def whole(h, a, b):
            return buf.at[h, slot(a, b)]

        def piece(h, a, b, p):
            return buf.at[h, slot(a, b), pl.ds(p * mid, mid), :]

        def go(h, ref, idx, to):
            send(ref, ref, s_sem.at[h, idx], r_sem.at[h, idx], to)

        def come(h, ref, idx, frm):
            recv(ref, s_sem.at[h, idx], r_sem.at[h, idx], frm)

        off = (0, -1, 1, 2)

        def spread(h, i):
            a, b, fn, fp, gn, gp, ff = parts(h)
            ref = whole(h, a + off[i] + 4, b)
            go(h, ref, 4 + i, gn)
            go(h, ref, 8 + i, gp)

        def start(hs):
            for h in hs:
                a, b, fn, fp, gn, gp, ff = parts(h)
                go(h, whole(h, a, b), 0, fn)
                go(h, whole(h, a, b), 1, fp)
                go(h, whole(h, a, b), 2, ff)
            for h in hs:
                spread(h, 0)

        def near():
            for h in (0, 1):
                a, b, fn, fp, gn, gp, ff = parts(h)
                come(h, whole(h, a + 3, b), 0, fp)
                come(h, whole(h, a + 1, b), 1, fn)
            for h in (0, 1):
                spread(h, 1)
                spread(h, 2)

        def far():
            for h in (0, 1):
                a, b, fn, fp, gn, gp, ff = parts(h)
                come(h, whole(h, a + 2, b), 2, ff)
                spread(h, 3)

        def across(i):
            for h in (0, 1):
                a, b, fn, fp, gn, gp, ff = parts(h)
                aa = a + off[i] + 4
                come(h, whole(h, aa, b + 3), 4 + i, gp)
                go(h, piece(h, aa, b + 3, 0), 12 + i, gn)
                come(h, whole(h, aa, b + 1), 8 + i, gn)
                go(h, piece(h, aa, b + 1, 1), 16 + i, gp)

        def last(i):
            for h in (0, 1):
                a, b, fn, fp, gn, gp, ff = parts(h)
                aa = a + off[i] + 4
                come(h, piece(h, aa, b + 2, 0), 12 + i, gp)
                come(h, piece(h, aa, b + 2, 1), 16 + i, gn)

        return start, near, far, across, last

    a_start, a_near, a_far, a_across, a_last = gather_steps(wbuf.at[zh], s_w.at[0], r_w.at[0])
    b_start, b_near, b_far, b_across, b_last = gather_steps(wbuf.at[1 - zh], s_w.at[1], r_w.at[1])

    turn = lax.broadcasted_iota(jnp.int32, (128, 256), 0) + lax.broadcasted_iota(jnp.int32, (128, 256), 1)
    turn = jnp.where(turn == 128, 1.0, 0.0).astype(BF)
    taps = taps_ref[...]
    taps_high = taps.astype(BF)
    taps_low = (taps - taps_high.astype(F32)).astype(BF)
    base[...] = jnp.dot(taps_high, turn, preferred_element_type=F32) + jnp.dot(
        taps_low, turn, preferred_element_type=F32
    )

    def build(g, _):
        row = jnp.broadcast_to(base[pl.ds(g, 1), :], (UNIT, 256))
        rows = pl.ds(pl.multiple_of(g * UNIT, UNIT), UNIT)
        rolled = pltpu.roll(row, 0, 1, stride=1, stride_axis=0)
        high = rolled.astype(BF)
        thi[rows, :] = high
        tlo[rows, :] = (rolled - high.astype(F32)).astype(BF)
        return 0

    lax.fori_loop(0, CH // GROUP, build, 0, unroll=8)

    lane_group = lax.broadcasted_iota(jnp.int32, (UNIT, 128), 1) // GROUP
    per = 128 // GROUP

    unit_at = (HALF, HALF + UNIT, UNIT, 0)

    def convolve(u):
        lo = unit_at[u]
        window = slice(lo, lo + 256)

        def slab(i, _):
            rows = pl.ds(pl.multiple_of(i * per * UNIT, per * UNIT), per * UNIT)
            both = jnp.dot(thi[rows, :], ghl[i, window, :], preferred_element_type=F32)
            rest = jnp.dot(tlo[rows, :], ghl[i, window, :128], preferred_element_type=F32)
            both = both[:, :128] + both[:, 128:] + rest
            conv = both[:UNIT]
            for g in range(1, per):
                conv = jnp.where(lane_group == g, both[g * UNIT : (g + 1) * UNIT], conv)
            lanes = pl.ds(pl.multiple_of(i * 128, 128), 128)
            mixed = x1f[lo : lo + UNIT, lanes] * (conv + skip_ref[:, lanes] * gf[lo : lo + UNIT, lanes])
            mall[zh, zl, pl.ds(pl.multiple_of(core * TOK + lo, UNIT), UNIT), lanes] = mixed.astype(BF)
            return 0

        lax.fori_loop(0, CH // 128, slab, 0, unroll=8)

    def halo_ready(k):
        halo_recv(k)
        lo, count = halo[k]

        @pl.when(first)
        def _():
            ghl[:, lo : lo + count, :128] = jnp.zeros((CH // 128, count, 128), BF)

    def rows_of(zz, cc, lo, count):
        zz = zz % 8
        return mall.at[zz // 4, zz % 4, pl.ds(cc * TOK + lo, count), :]

    def unit(zz, cc, u):
        return rows_of(zz, cc, unit_at[u], UNIT)

    def pair(zz, cc, half):
        return rows_of(zz, cc, HALF * (1 - half), HALF)

    def square(zz, cc, half):
        zz = zz % 8
        at = pl.ds(pl.multiple_of(cc * TOK + HALF * (1 - half), HALF), HALF)
        m = mall[zz // 4, zz % 4, at, :].astype(F32)
        m = m * m
        total = m[:, :128]
        for i in range(1, CH // 128):
            total = total + m[:, i * 128 : (i + 1) * 128]
        psum[zz // 4, at, :] += total

    def hand_over(zz, idx, half):
        ref = pair(zz, core, half)
        send(ref, ref, s_oc.at[idx, half], r_oc.at[idx, half], other)

    def ring_own(u):
        convolve(u)
        own = unit(z, core, u)
        send(own, own, s_zp.at[0, u], r_zp.at[0, u], z_next)
        send(own, own, s_zm.at[0, u], r_zm.at[0, u], z_prev)

    def ring_own_rest(half):
        hand_over(z, 0, half)
        square(z, core, half)

    def ring_step(k, u):
        if k < 3 or u % 2 == 0:
            ref = unit(z + 7 - k, core, u)
            recv(ref, s_zp.at[k, u], r_zp.at[k, u], z_prev)
            if k + 1 < 3 or (k + 1 == 3 and u % 2 == 0):
                send(ref, ref, s_zp.at[k + 1, u], r_zp.at[k + 1, u], z_next)
        if k < 3 or u % 2 == 1:
            ref = unit(z + 1 + k, core, u)
            recv(ref, s_zm.at[k, u], r_zm.at[k, u], z_next)
            if k + 1 < 3 or (k + 1 == 3 and u % 2 == 1):
                send(ref, ref, s_zm.at[k + 1, u], r_zm.at[k + 1, u], z_prev)

    def ring_rest(k, half):
        hand_over(z + 7 - k, 1 + k, half)
        if k < 3:
            hand_over(z + 1 + k, 5 + k, half)
        square(z + 7 - k, core, half)
        if k < 3:
            square(z + 1 + k, core, half)

    def from_other(idx, half):
        step = (0, 7, 6, 5, 4, 1, 2, 3)[idx]
        recv(pair(z + step, 1 - core, half), s_oc.at[idx, half], r_oc.at[idx, half], other)
        square(z + step, 1 - core, half)

    def weights(zz, lanes):
        pieces = []
        for i in range(4):
            for zz_hi in (0, 1):
                pieces += [wbuf[zz_hi, 0, zz * 4 + i, :, lanes], wbuf[zz_hi, 1, i * 4 + zz, :, lanes]]
        return jnp.concatenate(pieces, axis=0)

    def keys_values(zhi):
        inv = lax.rsqrt(jnp.sum(psum[zhi], axis=-1, keepdims=True) * (1.0 / (4 * CH)) + 1e-06)
        proj = None
        for zz in range(4):
            rounded = (mall[zhi, zz].astype(F32) * inv * gain_ref[:, zz * CH : (zz + 1) * CH]).astype(BF)
            normed[zhi, zz] = rounded
            part = jnp.dot(rounded, weights(zz, slice(HD, 3 * HD)), preferred_element_type=F32)
            proj = part if proj is None else proj + part
        proj = proj.astype(BF).astype(F32)
        values = jnp.transpose(proj[:, HD:]).astype(BF)
        at = own_slot(zhi)
        kv[zhi, at, :256, :] = proj[:, :HD].astype(BF)
        kv[zhi, at, 256:384, :] = values[:, :128]
        kv[zhi, at, 384:, :] = values[:, 128:]

    def queries():
        for zhi in (0, 1):
            proj = None
            for zz in range(4):
                part = jnp.dot(normed[zhi, zz], weights(zz, slice(0, HD)), preferred_element_type=F32)
                proj = part if proj is None else proj + part
            qt[:, zhi * 256 : (zhi + 1) * 256] = jnp.transpose(proj.astype(BF).astype(F32)).astype(BF)

    scale = math.log2(math.e) / math.sqrt(HD)

    def scores_of(h, index):
        return jnp.dot(kv[h, index, :256, :], qt[...], preferred_element_type=F32) * scale

    def weigh(units, probs):
        values = jnp.concatenate(
            [kv[h, index, lo : lo + 128, :] for h, index in units for lo in (256, 384)], axis=1
        )
        probs = jnp.concatenate([p.astype(BF) for p in probs], axis=0)
        return jnp.dot(values, probs, preferred_element_type=F32)

    def total_of(probs):
        total = probs[0]
        for p in probs[1:]:
            total = total + p
        return jnp.sum(total, axis=0, keepdims=True)

    def absorb_own():
        units = [(h, own_slot(h)) for h in (0, 1)]
        q_pos = lax.broadcasted_iota(jnp.int32, (256, SUP), 1)
        k_pos = lax.broadcasted_iota(jnp.int32, (256, SUP), 0)
        scores = [jnp.where(k_pos + h * 256 <= q_pos, scores_of(h, index), -1e30) for h, index in units]
        top = scores[0]
        for t in scores[1:]:
            top = jnp.maximum(top, t)
        top = jnp.max(top, axis=0, keepdims=True)
        probs = [jnp.exp2(t - top) for t in scores]
        mrow[...] = top
        lsum[...] = total_of(probs)
        acc[...] = weigh(units, probs)

    def absorb(units):
        biases = [jnp.where(block < s, 0.0, -1e30) for _, _, block in units]
        units = [unit[:2] for unit in units]
        scores = [scores_of(*unit) for unit in units]
        old = mrow[...]
        top = old
        for t, bias in zip(scores, biases):
            top = jnp.maximum(top, jnp.max(t, axis=0, keepdims=True) + bias)
        probs = [jnp.exp2(t - (top - bias)) for t, bias in zip(scores, biases)]
        alpha = jnp.exp2(old - top)
        mrow[...] = top
        lsum[...] = lsum[...] * alpha + total_of(probs)
        acc[...] = acc[...] * alpha + weigh(units, probs)

    def arrived(places):
        units = []
        for h, da, db in places:
            a, b = (x, y) if h == 0 else (y, x)
            aa, bb = (a + da + 4) % 4, (b + db + 4) % 4
            units.append((h, bb * 4 + aa, bb * 4 + aa if h == 0 else aa * 4 + bb))
        seen = units[0][2] < s
        for unit in units[1:]:
            seen = seen | (unit[2] < s)

        @pl.when(seen)
        def _():
            absorb(units)

    weights_from(0)
    a_start((0, 1))
    first = c == 0
    recv(rim, s_halo.at[3], r_halo.at[3], c_prev)
    rest = rim[:, CH:].astype(F32)
    rest = jnp.concatenate([rest[2 * i : 2 * i + 2] for i in range(8)], axis=1)
    rows = jnp.concatenate([rim[:, :CH].astype(F32), rest], axis=0)
    rows = jnp.where(first, 0.0, rows)
    for i in range(3):
        ext[i, 10:16, :] = rows[6 * i : 6 * i + 6]
    gate_rows(0, 16)
    halo_send(2)
    x1_rows(0, 16)
    psum[...] = jnp.zeros_like(psum)
    halo_ready(0)
    ring_own(0)
    ring_own(1)
    halo_ready(1)
    ring_own(2)
    ring_own_rest(0)
    a_across(0)
    a_near()
    a_far()
    weights_from(1)
    weights_from(2)
    b_start((0, 1))
    ring_step(0, 0)
    ring_step(0, 1)
    halo_ready(2)
    ring_own(3)
    ring_step(0, 2)
    ring_own_rest(1)
    ring_rest(0, 0)
    from_other(0, 0)
    a_across(1)
    a_across(2)
    a_across(3)
    ring_step(1, 0)
    ring_step(1, 1)
    ring_step(0, 3)
    ring_rest(1, 0)
    ring_rest(0, 1)
    from_other(1, 0)
    from_other(5, 0)
    ring_step(1, 2)
    b_across(0)
    b_near()
    b_far()
    from_other(0, 1)
    ring_step(2, 0)
    ring_step(2, 1)
    ring_step(1, 3)
    ring_rest(2, 0)
    ring_rest(1, 1)
    for i in range(4):
        a_last(i)
    b_across(1)
    b_across(2)
    b_across(3)
    from_other(2, 0)
    from_other(6, 0)
    from_other(1, 1)
    from_other(5, 1)
    ring_step(2, 2)
    ring_step(3, 0)
    ring_step(3, 1)
    ring_step(2, 3)
    ring_rest(3, 0)
    ring_rest(2, 1)
    from_other(3, 0)
    from_other(7, 0)
    from_other(2, 1)
    from_other(6, 1)
    from_other(4, 0)
    from_other(3, 1)
    from_other(7, 1)
    for i in range(4):
        b_last(i)
    k_start, k_near, k_far, k_across, k_last = gather_steps(kv, s_kv, r_kv)
    keys_values(zh)
    k_start((zh,))
    ring_step(3, 2)
    ring_step(3, 3)
    ring_rest(3, 1)
    from_other(4, 1)
    keys_values(1 - zh)
    k_start((1 - zh,))
    queries()
    absorb_own()
    off = (0, -1, 1, 2)

    def across_arrived(i):
        for h in (0, 1):
            arrived([(h, off[i], -1), (h, off[i], 1)])

    k_across(0)
    k_near()
    k_far()
    across_arrived(0)
    for h in (0, 1):
        arrived([(h, -1, 0), (h, 1, 0)])
    k_across(1)
    k_across(2)
    arrived([(0, 2, 0), (1, 2, 0)])
    across_arrived(1)
    k_across(3)
    across_arrived(2)
    across_arrived(3)
    for i in range(4):
        k_last(i)
        arrived([(0, off[i], 2), (1, off[i], 2)])

    result = jnp.transpose(acc[...] / lsum[...]).astype(BF)
    for rr in range(4):
        att[rr] = result[rr * TOK : (rr + 1) * TOK]
    for k in (1, 2, 0):
        send(att.at[mate_rank[k]], oland.at[r], s_out.at[k], r_out.at[k], mates[k])
    oland[r] = att[r]
    for k in range(3):
        recv(oland.at[mate_rank[k]], s_out.at[k], r_out.at[k], mates[k])
    for rr in range(4):
        out_ref[:, rr * HD : (rr + 1) * HD] = oland[rr]
    for copy in pending:
        copy.wait_send()


def per_device(streams, short_taps, long_taps, skip_gain, norm_gain, w_qkv):
    vmem = pl.BlockSpec(memory_space=pltpu.VMEM)
    dma = pltpu.SemaphoreType.DMA
    return pl.pallas_call(
        kernel,
        out_shape=jax.ShapeDtypeStruct((TOK, 4 * HD), BF),
        in_specs=[pl.BlockSpec(memory_space=pl.ANY)] + [vmem] * 4 + [pl.BlockSpec(memory_space=pl.ANY)],
        out_specs=vmem,
        scratch_shapes=[
            pltpu.VMEM((3, TOK, CH), BF),
            pltpu.VMEM((3, 64, 4 * HD), BF),
            pltpu.VMEM((16, CH + 128), BF),
            pltpu.VMEM((16, CH + 128), BF),
            pltpu.VMEM((3, 16 + TOK, CH), F32),
            pltpu.VMEM((CH // 128, 2 * TOK + 96, 256), BF),
            pltpu.VMEM((TOK, CH), F32),
            pltpu.VMEM((TOK, CH), F32),
            pltpu.VMEM((64, 256), F32),
            pltpu.VMEM((CH // GROUP * UNIT, 256), BF),
            pltpu.VMEM((CH // GROUP * UNIT, 256), BF),
            pltpu.VMEM((2, 4, 256, CH), BF),
            pltpu.VMEM((4, 64, 3 * HD), BF),
            pltpu.VMEM((2, 2, 16, 64, 3 * HD), BF),
            pltpu.VMEM((2, 4, 256, CH), BF),
            pltpu.VMEM((2, 16, 512, HD), BF),
            pltpu.VMEM((HD, SUP), BF),
            pltpu.VMEM((HD, SUP), F32),
            pltpu.VMEM((1, SUP), F32),
            pltpu.VMEM((1, SUP), F32),
            pltpu.VMEM((2, 256, 128), F32),
            pltpu.VMEM((4, TOK, HD), BF),
            pltpu.VMEM((4, TOK, HD), BF),
            dma((2,)),
            dma((4,)), dma((4,)),
            dma((3,)), dma((3,)),
            dma((2, 2, 20)), dma((2, 2, 20)),
            dma((2, 20)), dma((2, 20)),
            dma((4, 4)), dma((4, 4)),
            dma((4, 4)), dma((4, 4)),
            dma((8, 2)), dma((8, 2)),
            dma((3,)), dma((3,)),
        ],
        compiler_params=pltpu.CompilerParams(
            collective_id=0, has_side_effects=True, vmem_limit_bytes=56 * 1024 * 1024
        ),
    )(
        streams,
        short_taps,
        long_taps,
        skip_gain.reshape(1, CH),
        norm_gain.reshape(1, 4 * CH),
        jnp.transpose(w_qkv, (1, 0, 2)),
    )


def solution(mesh):
    in_specs = (
        P(None, "ctx", "head"),
        P(None, None, "head"),
        P("head", None),
        P("head"),
        P(),
        P("ctx", None, "head"),
    )
    return jax.shard_map(
        per_device, mesh=mesh, in_specs=in_specs, out_specs=P("ctx", "head"), check_vma=False
    )
```

time: 93.4 us -> 85.5 us (0.915)
  Pallas kernels: 91.7 us -> 83.8 us
    pallas_call x1, Pallas kernels: 91.7 us -> 83.8 us  [per_device(): pl.pallas_call(kernel, out_shape=jax.ShapeDtypeStruct((TOK, 4 * HD), BF),...]
where the time goes in v2:
time: 85.5 us; the launch traced here: 85.4 us
  Pallas kernels  83.8 us (98%)
  local copies, waits for them, and re-layouts  1.57 us (2%)
    pallas_call x1, Pallas kernels, per_device(): pl.pallas_call(kernel, out_shape=jax.ShapeDtypeStruct((TOK, 4 * HD), BF),...  83.8 us

profile of v2, /device:TPU:1, one launch (start us, length us, event | category | flops | bytes accessed | tf_op | source)
XLA Modules:
  0.0 85.4 jit_solution(5204189345878933664)
XLA Ops:
  0.0 83.8 %shard_map.64 = bf16[128,512]{1,0:T(8,128)(2,1)} custom-call(bf16[3,128,1024]{2,1,0:T(8,128)(2,1)} %x_hbm.1, f32[3,7,1024]{2,1,0:T(8,128)} %st_ref.1, f32[64,128]{1,0:T(8,128)} %taps_ref.1, f32[1,1024]{1,0:T(1,128)} %bitcast.5, f32[1,4096]{1,0:T(1,128)} %bitcast.4, bf16[3,64,512]{2,1,0:T(8,128)(2,1)} %bitcast.3), custom_call_target="tpu_custom_call" | custom-call | tf_op jit(solution)/shard_map/pallas_call | solution.py:573
  83.8 1.6 %copy.8 = bf16[128,512]{1,0:T(8,128)(2,1)} copy(bf16[128,512]{1,0:T(8,128)(2,1)} %shard_map.64) | data formatting | bytes 262144

commit v3 on v2

--- a/solution.py
+++ b/solution.py
@@ -156,7 +156,7 @@
     lax.fori_loop(0, CH // 128, clear, 0)
     halo_send(1)
 
-    def gather_steps(buf, s_sem, r_sem):
+    def gather_steps(buf, s_sem, r_sem, relay=False):
         mid = buf.shape[2] // 2
 
         def parts(h):
@@ -200,7 +200,8 @@
                 a, b, fn, fp, gn, gp, ff = parts(h)
                 go(h, whole(h, a, b), 0, fn)
                 go(h, whole(h, a, b), 1, fp)
-                go(h, whole(h, a, b), 2, ff)
+                if not relay:
+                    go(h, whole(h, a, b), 2, ff)
             for h in hs:
                 spread(h, 0)
 
@@ -208,7 +209,11 @@
             for h in (0, 1):
                 a, b, fn, fp, gn, gp, ff = parts(h)
                 come(h, whole(h, a + 3, b), 0, fp)
+                if relay:
+                    go(h, piece(h, a + 3, b, 0), 2, fn)
                 come(h, whole(h, a + 1, b), 1, fn)
+                if relay:
+                    go(h, piece(h, a + 1, b, 1), 3, fp)
             for h in (0, 1):
                 spread(h, 1)
                 spread(h, 2)
@@ -216,7 +221,11 @@
         def far():
             for h in (0, 1):
                 a, b, fn, fp, gn, gp, ff = parts(h)
-                come(h, whole(h, a + 2, b), 2, ff)
+                if relay:
+                    come(h, piece(h, a + 2, b, 0), 2, fp)
+                    come(h, piece(h, a + 2, b, 1), 3, fn)
+                else:
+                    come(h, whole(h, a + 2, b), 2, ff)
                 spread(h, 3)
 
         def across(i):
@@ -519,7 +528,7 @@
     from_other(7, 1)
     for i in range(4):
         b_last(i)
-    k_start, k_near, k_far, k_across, k_last = gather_steps(kv, s_kv, r_kv)
+    k_start, k_near, k_far, k_across, k_last = gather_steps(kv, s_kv, r_kv, relay=True)
     keys_values(zh)
     k_start((zh,))
     ring_step(3, 2)

time: 85.5 us -> 84.2 us (0.985)
  Pallas kernels: 83.8 us -> 82.5 us
    pallas_call x1, Pallas kernels: 83.8 us -> 82.5 us  [per_device(): pl.pallas_call(kernel, out_shape=jax.ShapeDtypeStruct((TOK, 4 * HD), BF),...]
where the time goes in v3:
time: 84.2 us; the launch traced here: 84.1 us
  Pallas kernels  82.5 us (98%)
  local copies, waits for them, and re-layouts  1.57 us (2%)
    pallas_call x1, Pallas kernels, per_device(): pl.pallas_call(kernel, out_shape=jax.ShapeDtypeStruct((TOK, 4 * HD), BF),...  82.5 us

profile of v3, /device:TPU:1, one launch (start us, length us, event | category | flops | bytes accessed | tf_op | source)
XLA Modules:
  0.0 84.1 jit_solution(9836646039084262254)
XLA Ops:
  0.0 82.5 %shard_map.64 = bf16[128,512]{1,0:T(8,128)(2,1)} custom-call(bf16[3,128,1024]{2,1,0:T(8,128)(2,1)} %x_hbm.1, f32[3,7,1024]{2,1,0:T(8,128)} %st_ref.1, f32[64,128]{1,0:T(8,128)} %taps_ref.1, f32[1,1024]{1,0:T(1,128)} %bitcast.5, f32[1,4096]{1,0:T(1,128)} %bitcast.4, bf16[3,64,512]{2,1,0:T(8,128)(2,1)} %bitcast.3), custom_call_target="tpu_custom_call" | custom-call | tf_op jit(solution)/shard_map/pallas_call | solution.py:582
  82.5 1.6 %copy.8 = bf16[128,512]{1,0:T(8,128)(2,1)} copy(bf16[128,512]{1,0:T(8,128)(2,1)} %shard_map.64) | data formatting | bytes 262144

commit v4 on v3

--- a/solution.py
+++ b/solution.py
@@ -514,16 +514,12 @@
     from_other(1, 1)
     from_other(5, 1)
     ring_step(2, 2)
-    ring_step(3, 0)
-    ring_step(3, 1)
     ring_step(2, 3)
-    ring_rest(3, 0)
     ring_rest(2, 1)
     from_other(3, 0)
     from_other(7, 0)
     from_other(2, 1)
     from_other(6, 1)
-    from_other(4, 0)
     from_other(3, 1)
     from_other(7, 1)
     for i in range(4):
@@ -531,9 +527,13 @@
     k_start, k_near, k_far, k_across, k_last = gather_steps(kv, s_kv, r_kv, relay=True)
     keys_values(zh)
     k_start((zh,))
+    ring_step(3, 0)
+    ring_step(3, 1)
+    ring_rest(3, 0)
     ring_step(3, 2)
     ring_step(3, 3)
     ring_rest(3, 1)
+    from_other(4, 0)
     from_other(4, 1)
     keys_values(1 - zh)
     k_start((1 - zh,))

time: 84.2 us -> 84.2 us (level)
  no operation moved by 1% of the time
where the time goes in v4:
time: 84.2 us; the launch traced here: 84.1 us
  Pallas kernels  82.5 us (98%)
  local copies, waits for them, and re-layouts  1.57 us (2%)
    pallas_call x1, Pallas kernels, per_device(): pl.pallas_call(kernel, out_shape=jax.ShapeDtypeStruct((TOK, 4 * HD), BF),...  82.5 us

profile of v4, /device:TPU:1, one launch (start us, length us, event | category | flops | bytes accessed | tf_op | source)
XLA Modules:
  0.0 84.1 jit_solution(16801586938490282404)
XLA Ops:
  0.0 82.5 %shard_map.64 = bf16[128,512]{1,0:T(8,128)(2,1)} custom-call(bf16[3,128,1024]{2,1,0:T(8,128)(2,1)} %x_hbm.1, f32[3,7,1024]{2,1,0:T(8,128)} %st_ref.1, f32[64,128]{1,0:T(8,128)} %taps_ref.1, f32[1,1024]{1,0:T(1,128)} %bitcast.5, f32[1,4096]{1,0:T(1,128)} %bitcast.4, bf16[3,64,512]{2,1,0:T(8,128)(2,1)} %bitcast.3), custom_call_target="tpu_custom_call" | custom-call | tf_op jit(solution)/shard_map/pallas_call | solution.py:582
  82.5 1.6 %copy.8 = bf16[128,512]{1,0:T(8,128)(2,1)} copy(bf16[128,512]{1,0:T(8,128)(2,1)} %shard_map.64) | data formatting | bytes 262144

commit v5 on v4

--- a/solution.py
+++ b/solution.py
@@ -470,12 +470,12 @@
     halo_ready(1)
     ring_own(2)
     ring_own_rest(0)
+    weights_from(1)
+    weights_from(2)
+    b_start((0, 1))
     a_across(0)
     a_near()
     a_far()
-    weights_from(1)
-    weights_from(2)
-    b_start((0, 1))
     ring_step(0, 0)
     ring_step(0, 1)
     halo_ready(2)

time: 84.2 us -> 84.3 us (level)
  no operation moved by 1% of the time
where the time goes in v5:
time: 84.3 us; the launch traced here: 84.1 us
  Pallas kernels  82.6 us (98%)
  local copies, waits for them, and re-layouts  1.57 us (2%)
    pallas_call x1, Pallas kernels, per_device(): pl.pallas_call(kernel, out_shape=jax.ShapeDtypeStruct((TOK, 4 * HD), BF),...  82.6 us

profile of v5, /device:TPU:1, one launch (start us, length us, event | category | flops | bytes accessed | tf_op | source)
XLA Modules:
  0.0 84.1 jit_solution(998518093198622948)
XLA Ops:
  0.0 82.6 %shard_map.64 = bf16[128,512]{1,0:T(8,128)(2,1)} custom-call(bf16[3,128,1024]{2,1,0:T(8,128)(2,1)} %x_hbm.1, f32[3,7,1024]{2,1,0:T(8,128)} %st_ref.1, f32[64,128]{1,0:T(8,128)} %taps_ref.1, f32[1,1024]{1,0:T(1,128)} %bitcast.5, f32[1,4096]{1,0:T(1,128)} %bitcast.4, bf16[3,64,512]{2,1,0:T(8,128)(2,1)} %bitcast.3), custom_call_target="tpu_custom_call" | custom-call | tf_op jit(solution)/shard_map/pallas_call | solution.py:582
  82.6 1.6 %copy.8 = bf16[128,512]{1,0:T(8,128)(2,1)} copy(bf16[128,512]{1,0:T(8,128)(2,1)} %shard_map.64) | data formatting | bytes 262144
